TPU v7x, 512 devices: a whole 4x8x8 slice. The times are simulated.
512 devices in a mesh: users: 16 (over y_lo, x), items: 32 (over z, y_hi, core).
Axes of the slice: x: 4, y: 8 (y_hi: 2, y_lo: 4; y = y_hi * 4 + y_lo), z: 8, core: 2. Of those that a mesh axis runs over, the one named last changes fastest.
Arguments:
- histories: int32 [16, 256], replicated, may hold values from 0 to 1048575
- item_degree: int32 [1048576], P('items'), may hold values from 1 to 63
- user_degree: int32 [131072], P('users'), may hold values from 1 to 63
- tile_values: float32 [16, 32, 24, 128, 128], P('users', 'items'), may hold values from 0 to 1
- tile_rows: int32 [16, 32, 24], P('users', 'items'), may hold values from 0 to 63
- tile_cols: int32 [16, 32, 24], P('users', 'items'), may hold values from 0 to 255
- tile_count: int32 [16, 32], P('users', 'items'), may hold values from 1 to 24, as said below
Outputs:
- scores: float32 [16, 1048576], P('users', 'items')
Inputs may be any that keep to these rules, and one draw needn't show every extreme that they name: `tile_count`: every device has 1 to 24 live slots, and some device has exactly 24.
All inputs are finite; a program needn't handle non-finite values.
Results may differ from a plain program's by a relative error of at most 0.0003.
Values sent between devices are 32-bit elements; how exact they have to be, the bound alone decides.
A program may use at most 64 MiB of HBM per device.

v0:
```python
import jax
import jax.numpy as jnp
from jax import lax
from jax.sharding import PartitionSpec as P


def body(histories, item_degree, user_degree, tile_values, tile_rows, tile_cols, tile_count):
    highest = lax.Precision.HIGHEST
    queries = histories.shape[0]
    items_local = item_degree.shape[0]
    users_local = user_degree.shape[0]
    width = tile_values.shape[-1]
    item_blocks = items_local // width
    user_blocks = users_local // width
    values_now = tile_values[0, 0]
    block_rows = tile_rows[0, 0]
    block_cols = tile_cols[0, 0]
    slot_ids = jnp.arange(values_now.shape[0], dtype=jnp.int32)
    alive_mask = (slot_ids < tile_count[0, 0]).astype(jnp.float32)
    offset = lax.axis_index("items") * items_local
    local_ids = histories - offset
    inside = (local_ids >= 0) & (local_ids < items_local)
    query_ids = jnp.broadcast_to(jnp.arange(queries, dtype=jnp.int32)[:, None], histories.shape)
    hits = (
        jnp.zeros((queries, items_local), jnp.float32)
        .at[query_ids, jnp.clip(local_ids, 0, items_local - 1)]
        .add(jnp.where(inside, 1.0, 0.0))
    )
    item_scale = lax.rsqrt(item_degree.astype(jnp.float32))
    panels = (hits * item_scale[None, :]).reshape(queries, item_blocks, width)
    picked = jnp.take(panels, block_cols, axis=1)
    partial_value = jnp.einsum("qtk,tjk->qtj", picked, values_now, precision=highest)
    row_onehot = (block_rows[:, None] == jnp.arange(user_blocks, dtype=jnp.int32)[None, :]).astype(
        jnp.float32
    ) * alive_mask[:, None]
    user_terms = jnp.einsum("qtj,tu->quj", partial_value, row_onehot, precision=highest)
    user_scale = (1.0 / user_degree.astype(jnp.float32)).reshape(user_blocks, width)
    user_totals = lax.psum(user_terms, "items")
    weighted = user_totals * user_scale[None, :, :]
    picked_users = jnp.take(weighted, block_rows, axis=1)
    score_part = jnp.einsum("qtj,tjk->qtk", picked_users, values_now, precision=highest)
    block_range = jnp.arange(item_blocks, dtype=jnp.int32)
    col_onehot = (block_cols[:, None] == block_range[None, :]).astype(jnp.float32) * alive_mask[
        :, None
    ]
    score_terms = jnp.einsum("qtk,tb->qbk", score_part, col_onehot, precision=highest).reshape(
        queries, items_local
    )
    score_totals = lax.psum(score_terms, "users")
    count = queries // lax.axis_size("users")
    score_rows = lax.dynamic_slice_in_dim(score_totals, lax.axis_index("users") * count, count, 0)
    return score_rows * item_scale[None, :]


def solution(mesh):
    in_specs = (
        P(),
        P("items"),
        P("users"),
        P("users", "items", None, None, None),
        P("users", "items", None),
        P("users", "items", None),
        P("users", "items"),
    )
    out_specs = P("users", "items")
    return jax.shard_map(body, mesh=mesh, in_specs=in_specs, out_specs=out_specs, check_vma=False)
```

profile of v0, /device:TPU:2, one launch (start us, length us, event | category | flops | bytes accessed | tf_op | source)
XLA Modules:
  0.0 588.5 jit_solution(13323144484975118217)
XLA Ops:
  6.5 0.0 copy-start
  6.5 0.0 all-reduce.3.cloned.1.call-start
  6.5 0.8 fusion.25
  7.4 0.7 select_bitcast_fusion.1
  8.1 0.7 fusion.34
  8.8 0.7 compare_and_fusion
  9.4 0.7 multiply_reduce_fusion
  10.2 0.7 and_reduce_fusion
  10.9 29.4 %scatter_custom_fusion = f32[524288]{0:T(1024)} fusion(s32[4096]{0:T(1024)S(1)} %bitcast.65, f32[4096]{0:T(1024)S(1)} %bitcast.66, f32[]{:T(128)} %constant.18.clone.1), kind=kCustom, calls=%fused_computation.13 | custom fusion | flops 4096 | bytes 2097156
  40.3 0.0 copy-start.1
  40.3 2.8 reshape.100
  43.1 0.0 copy-done.1
  43.8 3.1 copy_bitcast_fusion.1
  46.9 0.0 copy-start.3
  46.9 0.0 copy-start.2
  46.9 2.2 gather_fusion
  49.1 0.0 copy-done
  49.1 2.6 fusion.4
  51.7 0.0 copy-done.3
  51.7 1.5 convolution_bitcast_fusion
  53.2 0.0 all-reduce.3.cloned.1.call-update
  53.2 0.0 all-reduce.5.cloned.1.call-start
  53.3 0.0 copy-done.2
  53.4 0.0 copy-start.4
  53.4 347.5 %all-reduce.3.cloned.1.call-done = f32[16,64,128]{2,1,0:T(8,128)} async-done(((f32[16,64,128]{2,1,0:T(8,128)}), f32[16,64,128]{2,1,0:T(8,128)}) %all-reduce.3.cloned.1.call-update) | async-done | bytes 524304 | tf_op jit(solution)/shard_map/psum | solution.py:38
  400.9 1.1 broadcast_multiply_fusion
  402.0 0.3 copy.16
  402.3 0.6 gather_fusion.1
  402.9 1.5 fusion.7
  404.4 0.0 copy-done.4
  404.4 1.9 fusion.14
  406.3 2.5 copy.28
  408.8 0.0 all-reduce.5.cloned.1.call-update
  408.8 170.8 %all-reduce.5.cloned.1.call-done = f32[16,32768]{1,0:T(8,128)} async-done(((f32[16,32768]{1,0:T(8,128)}), f32[16,32768]{1,0:T(8,128)}) %all-reduce.5.cloned.1.call-update) | async-done | bytes 2097168 | tf_op jit(solution)/shard_map/psum | solution.py:49
  579.7 2.0 dynamic-slice_multiply_fusion
  (11 shorter events, 0.1 us)
Async XLA Ops:
  6.5 42.6 %copy-start = (f32[1,1,24,128,128]{4,3,2,1,0:T(8,128)S(1)}, f32[1,1,24,128,128]{4,3,2,1,0:T(8,128)}, u32[]{:S(2)}) copy-start(f32[1,1,24,128,128]{4,3,2,1,0:T(8,128)} %param.10) | copy-start | bytes 4718596
  6.5 394.4 %all-reduce.3.cloned.1.call-start = ((), (), s32[]{:S(2)}) async-start(), calls=%async_computation | async-start | bytes 1048576 | tf_op jit(solution)/shard_map/psum | solution.py:38
  40.3 2.8 copy-start.1
  46.9 4.8 copy-start.3
  46.9 6.4 %copy-start.2 = (s32[8192]{0:T(1024)S(1)}, s32[8192]{0:T(1024)}, u32[]{:S(2)}) copy-start(s32[8192]{0:T(1024)} %param.9) | copy-start | bytes 98308
  53.2 526.4 %all-reduce.5.cloned.1.call-start = ((), (), s32[]{:S(2)}) async-start(), calls=%async_computation.1 | async-start | bytes 4194304 | tf_op jit(solution)/shard_map/psum | solution.py:49
  53.4 351.0 %copy-start.4 = (s32[1,1,24]{2,1,0:T(1,128)S(1)}, s32[1,1,24]{2,1,0:T(1,128)}, u32[]{:S(2)}) copy-start(s32[1,1,24]{2,1,0:T(1,128)} %param.12) | copy-start | bytes 292
Sparse Core Ops, SparseCore 0:
  53.4 347.4 all-reduce.2
  409.0 170.6 all-reduce.4
where the time goes:
time: 589 us
  waiting for transfers between devices  518 us (88%)
  other arithmetic  40 us (7%)
  between operations  14.2 us (2%)
  local copies, waits for them, and re-layouts  8.42 us (1%)
  matrix products  7.49 us (1%)
    psum x1, waiting for transfers between devices, body(): user_totals = lax.psum(user_terms, 'items')  348 us
    psum x1, waiting for transfers between devices, body(): score_totals = lax.psum(score_terms, 'users')  171 us
    unnamed x5, other arithmetic  31.6 us
  transfers between devices with their start and end apart: 2, of which 2 were waited for; matrix products, arithmetic and copies ran while one was open for 0% of the time, Pallas kernels for 0%

commit v1 on v0

--- a/solution.py
+++ b/solution.py
@@ -2,6 +2,8 @@
 import jax.numpy as jnp
 from jax import lax
 from jax.sharding import PartitionSpec as P
+
+follow_target = lambda mine, row_axis: jnp.sum(jax.lax.all_gather(mine, row_axis), axis=0)
 
 
 def body(histories, item_degree, user_degree, tile_values, tile_rows, tile_cols, tile_count):
@@ -35,7 +37,7 @@
     ) * alive_mask[:, None]
     user_terms = jnp.einsum("qtj,tu->quj", partial_value, row_onehot, precision=highest)
     user_scale = (1.0 / user_degree.astype(jnp.float32)).reshape(user_blocks, width)
-    user_totals = lax.psum(user_terms, "items")
+    user_totals = follow_target(user_terms, "items")
     weighted = user_totals * user_scale[None, :, :]
     picked_users = jnp.take(weighted, block_rows, axis=1)
     score_part = jnp.einsum("qtj,tjk->qtk", picked_users, values_now, precision=highest)

time: 589 us -> 444 us (0.75)
  waiting for transfers between devices: 518 us -> 368 us
  other arithmetic: 40 us -> 46.7 us
    psum x1 -> x0, waiting for transfers between devices: 348 us -> none  [body(): user_totals = lax.psum(user_terms, 'items')]
    all_gather x0 -> x1, waiting for transfers between devices: none -> 200 us  [jax.lax.all_gather(mine, row_axis)]
    reduce_sum x0 -> x1, other arithmetic: none -> 7.45 us  [jnp.sum(jax.lax.all_gather(mine, row_axis), axis=0)]
where the time goes in v1:
time: 444 us
  waiting for transfers between devices  368 us (83%)
  other arithmetic  46.7 us (11%)
  between operations  14.2 us (3%)
  local copies, waits for them, and re-layouts  8.11 us (2%)
  matrix products  7.46 us (2%)
    all_gather x1, waiting for transfers between devices, jax.lax.all_gather(mine, row_axis)  200 us
    psum x1, waiting for transfers between devices, body(): score_totals = lax.psum(score_terms, 'users')  168 us
    unnamed x5, other arithmetic  31.6 us
  transfers between devices with their start and end apart: 2, of which 2 were waited for; matrix products, arithmetic and copies ran while one was open for 0% of the time, Pallas kernels for 0%

profile of v1, /device:TPU:2, one launch (start us, length us, event | category | flops | bytes accessed | tf_op | source)
XLA Modules:
  0.0 444.1 jit_solution(17921575302995927580)
XLA Ops:
  6.5 0.0 copy-start
  6.5 0.0 all-gather.3.cloned.1.call-start
  6.5 0.8 fusion.25
  7.4 0.7 select_bitcast_fusion.1
  8.1 0.7 fusion.34
  8.8 0.7 compare_and_fusion
  9.4 0.7 multiply_reduce_fusion
  10.2 0.7 and_reduce_fusion
  10.9 29.4 %scatter_custom_fusion = f32[524288]{0:T(1024)} fusion(s32[4096]{0:T(1024)S(1)} %bitcast.67, f32[4096]{0:T(1024)S(1)} %bitcast.68, f32[]{:T(128)} %constant.18.clone.1), kind=kCustom, calls=%fused_computation.13 | custom fusion | flops 4096 | bytes 2097156
  40.3 0.0 copy-start.1
  40.3 2.8 reshape.100
  43.1 0.0 copy-done.1
  43.8 3.1 copy_bitcast_fusion.1
  46.9 0.0 copy-start.3
  46.9 0.0 copy-start.2
  46.9 2.2 gather_fusion
  49.1 0.0 copy-done
  49.1 2.6 fusion.4
  51.7 0.0 copy-done.3
  51.7 1.5 convolution_bitcast_fusion
  53.2 0.0 all-gather.3.cloned.1.call-update
  53.2 0.0 all-reduce.2.cloned.1.call-start
  53.3 0.0 copy-done.2
  53.4 199.8 %all-gather.3.cloned.1.call-done = f32[512,64,128]{2,1,0:T(8,128)} async-done(((f32[16,64,128]{2,1,0:T(8,128)}), f32[512,64,128]{2,1,0:T(8,128)}) %all-gather.3.cloned.1.call-update) | async-done | bytes 16777232 | tf_op jit(solution)/shard_map/all_gather | solution.py:6
  253.2 7.5 %reduce_sum.9 = f32[16,64,128]{2,1,0:T(8,128)S(1)} reduce(f32[32,16,64,128]{3,2,1,0:T(8,128)} %bitcast.63, f32[]{:T(128)} %constant.18.clone.1), dimensions={0}, to_apply=%region_1.2 | reduce | flops 4063232 | bytes 17301508 | tf_op jit(solution)/shard_map/reduce_sum | solution.py:6
  260.6 0.0 copy-start.4
  260.7 0.3 copy_multiply_fusion
  261.0 0.6 gather_fusion.1
  261.6 1.5 fusion.7
  263.0 0.0 copy-done.4
  263.1 1.9 fusion.14
  265.0 2.5 copy.26
  267.5 0.0 all-reduce.2.cloned.1.call-update
  267.5 167.7 %all-reduce.2.cloned.1.call-done = f32[16,32768]{1,0:T(8,128)} async-done(((f32[16,32768]{1,0:T(8,128)}), f32[16,32768]{1,0:T(8,128)}) %all-reduce.2.cloned.1.call-update) | async-done | bytes 2097168 | tf_op jit(solution)/shard_map/psum | solution.py:51
  435.2 2.0 dynamic-slice_multiply_fusion
  (11 shorter events, 0.1 us)
Async XLA Ops:
  6.5 42.6 %copy-start = (f32[1,1,24,128,128]{4,3,2,1,0:T(8,128)S(1)}, f32[1,1,24,128,128]{4,3,2,1,0:T(8,128)}, u32[]{:S(2)}) copy-start(f32[1,1,24,128,128]{4,3,2,1,0:T(8,128)} %param.10) | copy-start | bytes 4718596
  6.5 246.6 %all-gather.3.cloned.1.call-start = ((), (), s32[]{:S(2)}) async-start(), calls=%async_computation.1 | async-start | bytes 17301504 | tf_op jit(solution)/shard_map/all_gather | solution.py:6
  40.3 2.8 copy-start.1
  46.9 4.8 %copy-start.3 = (s32[1,1,24]{2,1,0:T(1,128)S(1)}, s32[1,1,24]{2,1,0:T(1,128)}, u32[]{:S(2)}) copy-start(s32[1,1,24]{2,1,0:T(1,128)} %param.11) | copy-start | bytes 292
  46.9 6.4 %copy-start.2 = (s32[8192]{0:T(1024)S(1)}, s32[8192]{0:T(1024)}, u32[]{:S(2)}) copy-start(s32[8192]{0:T(1024)} %param.9) | copy-start | bytes 98308
  53.2 382.0 %all-reduce.2.cloned.1.call-start = ((), (), s32[]{:S(2)}) async-start(), calls=%async_computation | async-start | bytes 4194304 | tf_op jit(solution)/shard_map/psum | solution.py:51
  260.6 2.4 copy-start.4
Sparse Core Ops, SparseCore 0:
  53.4 199.7 all-gather.2
  267.6 167.5 all-reduce.1
